TPU v7x, 128 devices: a whole 4x4x4 slice. The times are simulated.
128 devices in a mesh: group: 8 (over z, y_hi), member: 16 (over y_lo, x, core).
Axes of the slice: x: 4, y: 4 (y_hi: 2, y_lo: 2; y = y_hi * 2 + y_lo), z: 4, core: 2. Of those that a mesh axis runs over, the one named last changes fastest.
Arguments:
- raw_strain: float32 [5120, 4160], P(('group', 'member')), may hold values from -6 to 6
- fir_taps: float32 [64], replicated, may hold values from -0.75 to 0.75
- block_slot: int32 [5120], P(('group', 'member')), may hold values from 0 to 39, as said below
- pairings: int32 [2, 8], P(None, 'group'), may hold values from 0 to 7, as said below
- pair_subset: int32 [2, 16, 1], P(None, 'member'), may hold values from 0 to 15, as said below
Outputs:
- correlations: bfloat16 [2, 1, 5120, 40, 2048], P(None, None, ('group', 'member'))
Inputs may be any that keep to these rules, and one draw needn't show every extreme that they name: `block_slot`: the 40 entries of each block are a permutation of 0 to 39. Each row pairs the groups: pairings[r, pairings[r, g]] = g and pairings[r, g] != g; the rows are different rounds of one round-robin tournament. `pair_subset`: in each round, each member's 1 entries are different, and each member index is named by exactly 1 of the 16 rows.
All inputs are finite; a program needn't handle non-finite values.
Results may differ from a plain program's by a relative error of at most 0.006.
Values may be sent and summed in bfloat16 or wider, within the bound.
A program may use at most 128 MiB of HBM per device.

v0:
```python
import functools
import math

import jax
import jax.numpy as jnp
import ml_dtypes
import numpy as np
from jax import lax
from jax.experimental import pallas as pl
from jax.experimental.pallas import tpu as pltpu
from jax.sharding import PartitionSpec as P

SEG = 2048
TAPS = 64
NFFT = 4096
F0 = 24
NBIN = 1024
WIN = 64
LAG = 1024
ROUNDS = 2
KSUB = 1
CH = 40
RAW = 4160
EPS = 1e-06

PIECE = 256
PIECES = SEG // PIECE
SPAN = 640
OWN_STEP = 8
MIB = 1 << 20
BF16 = jnp.bfloat16
F32 = jnp.float32


def split_bf16(table):
    high = table.astype(ml_dtypes.bfloat16)
    low = (table - high.astype(np.float64)).astype(ml_dtypes.bfloat16)
    return high, low


def forward_tables():
    bins = F0 + np.arange(NBIN)
    phases = np.arange(PIECE)[:, None] * bins[None, :] % NFFT * (2.0 * math.pi / NFFT)
    high, low = split_bf16(np.concatenate([np.cos(phases), -np.sin(phases)], axis=1))
    shift = np.arange(PIECES)[:, None] * PIECE * bins[None, :] % NFFT * (2.0 * math.pi / NFFT)
    return high, low, np.cos(shift).astype(np.float32), -np.sin(shift).astype(np.float32)


def lag_tables():
    bins = F0 + np.arange(NBIN)
    phases = bins[:, None] * (2 * np.arange(LAG) + 1)[None, :] % (2 * NFFT) * (math.pi / NFFT)
    scale = 1.0 / math.sqrt(NBIN)
    cosine = (np.cos(phases) * scale).astype(ml_dtypes.bfloat16)
    sine = (-np.sin(phases) * scale).astype(ml_dtypes.bfloat16)
    half = bins * (math.pi / NFFT)
    turn = np.stack([np.cos(half), -np.sin(half)]).astype(np.float32)
    flip = np.eye(256)[::-1].astype(ml_dtypes.bfloat16)
    return cosine, sine, turn, flip


def dot(a, b):
    return jnp.dot(a, b, preferred_element_type=F32)


def parts(x):
    high = x.astype(BF16)
    return high, (x - high.astype(F32)).astype(BF16)


def whiten_kernel(raw_ref, taps_ref, slot_ref, high_ref, low_ref, tc_ref, ts_ref, panel_ref, dh_ref, dl_ref, re_ref, im_ref):
    taps = jnp.concatenate([taps_ref[...], jnp.zeros((1, SPAN - 128), F32)], axis=1)
    filter_rows = pltpu.roll(jnp.broadcast_to(taps, (PIECE, SPAN)), 0, 1, stride=2, stride_axis=0)
    pieces = [raw_ref[:, 2 * PIECE * b : 2 * PIECE * b + SPAN] for b in range(PIECES - 1)]
    last = raw_ref[:, 2 * PIECE * (PIECES - 1) :]
    pieces.append(jnp.concatenate([last, jnp.zeros((CH, SPAN - last.shape[1]), F32)], axis=1))
    xh, xl = parts(jnp.concatenate(pieces, axis=0))
    fh, fl = parts(filter_rows)
    contract = functools.partial(
        lax.dot_general, dimension_numbers=(((1,), (1,)), ((), ())), preferred_element_type=F32
    )
    dh, dl = parts(contract(xh, fh) + contract(xl, fh) + contract(xh, fl))
    dh_ref[...] = dh
    dl_ref[...] = dl
    width = 256
    for n in range(NBIN // width):
        cols = slice(width * n, width * (n + 1))
        both = []
        for base in (0, NBIN):
            at = slice(base + width * n, base + width * (n + 1))
            wide = dh_ref[...]
            both.append(dot(wide, high_ref[:, at]) + dot(dl_ref[...], high_ref[:, at]) + dot(wide, low_ref[:, at]))
        yr, yi = both
        re = jnp.zeros((CH, width), F32)
        im = jnp.zeros((CH, width), F32)
        for b in range(PIECES):
            tc = tc_ref[b : b + 1, cols]
            ts = ts_ref[b : b + 1, cols]
            r, i = yr[CH * b : CH * (b + 1)], yi[CH * b : CH * (b + 1)]
            re += r * tc - i * ts
            im += r * ts + i * tc
        re_ref[:, cols] = re
        im_ref[:, cols] = im
    re, im = re_ref[...], im_ref[...]
    total = re * re + im * im
    for step in (1, 2, 4, 8, 16, 32):
        total = total + pltpu.roll(total, NBIN - step, 1)
    total = pltpu.roll(total, WIN // 2, 1)
    col = lax.broadcasted_iota(jnp.int32, (CH, NBIN), 1)
    first, final = WIN // 2, NBIN - WIN // 2
    total = jnp.where(col < first, total[:, first : first + 1], total)
    total = jnp.where(col > final, total[:, final : final + 1], total)
    inverse = lax.rsqrt(total * (1.0 / WIN) + EPS)
    place = (lax.broadcasted_iota(jnp.int32, (CH, CH), 0) == slot_ref[...]).astype(F32).astype(BF16)
    panel_ref[:, :NBIN] = dot(place, (re * inverse).astype(BF16)).astype(BF16)
    panel_ref[:, NBIN:] = dot(place, (im * inverse).astype(BF16)).astype(BF16)


def correlate_kernel(own_ref, their_ref, cos_ref, sin_ref, turn_ref, flip_ref, out_ref, cre_ref, cim_ref):
    br = their_ref[0, :, :NBIN].astype(F32)
    bi = their_ref[0, :, NBIN:].astype(F32)
    tr, ti = turn_ref[0:1, :], turn_ref[1:2, :]
    own = own_ref[...].astype(F32)
    ar0, ai0 = own[:, :NBIN], own[:, NBIN:]
    ar = ar0 * tr - ai0 * ti
    ai = ar0 * ti + ai0 * tr
    for i in range(0, OWN_STEP, 2):
        res, ims = [], []
        for k in (i, i + 1):
            r, m = ar[k : k + 1], ai[k : k + 1]
            res.append(r * br + m * bi)
            ims.append(m * br - r * bi)
        rows = slice(CH * i, CH * (i + 2))
        cre_ref[rows, :] = jnp.concatenate(res, axis=0).astype(BF16)
        cim_ref[rows, :] = jnp.concatenate(ims, axis=0).astype(BF16)
    width = 256
    for n in range(LAG // width):
        cols = slice(width * n, width * (n + 1))
        even = dot(cre_ref[...], cos_ref[:, cols])
        odd = dot(cim_ref[...], sin_ref[:, cols])
        out_ref[:, LAG + width * n : LAG + width * (n + 1)] = (even + odd).astype(BF16)
        mirrored = dot((even - odd).astype(BF16), flip_ref[...])
        out_ref[:, LAG - width * (n + 1) : LAG - width * n] = mirrored.astype(BF16)


def whiten(raw_strain, fir_taps, block_slot):
    high, low, tc, ts = forward_tables()
    taps = jnp.pad(fir_taps, (0, 128 - TAPS)).reshape(1, 128)
    return pl.pallas_call(
        whiten_kernel,
        out_shape=jax.ShapeDtypeStruct((CH, 2 * NBIN), BF16),
        in_specs=[pl.BlockSpec(memory_space=pltpu.VMEM)] * 7,
        out_specs=pl.BlockSpec(memory_space=pltpu.VMEM),
        scratch_shapes=[pltpu.VMEM((PIECES * CH, PIECE), BF16)] * 2 + [pltpu.VMEM((CH, NBIN), F32)] * 2,
        compiler_params=pltpu.CompilerParams(vmem_limit_bytes=48 * MIB),
    )(raw_strain, taps, block_slot.reshape(1, CH), high, low, tc, ts)


def correlate(own, theirs):
    cosine, sine, turn, flip = lag_tables()
    rows = OWN_STEP * CH
    steps = CH // OWN_STEP
    whole = lambda r, i: (0, 0)
    return pl.pallas_call(
        correlate_kernel,
        grid=(ROUNDS, steps),
        out_shape=jax.ShapeDtypeStruct((ROUNDS * CH * CH, 2 * LAG), BF16),
        in_specs=[
            pl.BlockSpec((OWN_STEP, 2 * NBIN), lambda r, i: (i, 0)),
            pl.BlockSpec((1, CH, 2 * NBIN), lambda r, i: (r, 0, 0)),
            pl.BlockSpec((NBIN, LAG), whole),
            pl.BlockSpec((NBIN, LAG), whole),
            pl.BlockSpec((2, NBIN), whole),
            pl.BlockSpec((256, 256), whole),
        ],
        out_specs=pl.BlockSpec((rows, 2 * LAG), lambda r, i: (r * steps + i, 0)),
        scratch_shapes=[pltpu.VMEM((rows, NBIN), BF16)] * 2,
        compiler_params=pltpu.CompilerParams(vmem_limit_bytes=48 * MIB),
    )(own, theirs, cosine, sine, turn, flip)


def per_device(raw_strain, fir_taps, block_slot, pairings, pair_subset):
    panel = whiten(raw_strain, fir_taps, block_slot)
    mine = lax.all_gather(panel, "member", axis=0)
    picked = jnp.stack(
        [lax.dynamic_index_in_dim(mine, pair_subset[r, 0, 0], 0, keepdims=False) for r in range(ROUNDS)]
    )
    around = lax.all_gather(picked, "group", axis=0)
    theirs = jnp.stack(
        [lax.dynamic_index_in_dim(around, pairings[r, 0], 0, keepdims=False)[r] for r in range(ROUNDS)]
    )
    result = correlate(panel, theirs)
    return result.reshape(ROUNDS, KSUB, CH, CH, 2 * LAG)


def solution(mesh):
    in_specs = (
        P(("group", "member"), None),
        P(),
        P(("group", "member")),
        P(None, "group"),
        P(None, "member", None),
    )
    out_specs = P(None, None, ("group", "member"), None, None)
    return jax.shard_map(
        per_device, mesh=mesh, in_specs=in_specs, out_specs=out_specs, check_vma=False
    )
```

profile of v0, /device:TPU:0, one launch (start us, length us, event | category | flops | bytes accessed | tf_op | source)
XLA Modules:
  0.0 148.0 jit_solution(2596497566037140845)
XLA Ops:
  6.5 0.0 copy-start.10
  6.5 0.0 copy-start.11
  6.5 0.0 all-gather.5.cloned.1.call-start
  6.5 0.7 pad_bitcast_fusion.taps_ref
  7.2 0.0 copy-start.2
  7.2 1.2 copy-done.2
  8.4 0.0 copy-start.3
  8.5 1.2 copy-done.3
  9.7 0.0 copy-start.4
  9.7 1.1 copy-done.4
  10.8 0.0 copy-start.6
  10.8 0.8 copy-done.6
  11.5 0.0 copy-start.7
  11.5 0.8 copy-done.7
  12.3 0.0 copy-start.9
  12.3 0.7 copy-done.9
  12.9 0.0 copy-start
  12.9 0.0 copy-start.5
  12.9 0.0 copy-start.8
  12.9 4.1 %shard_map.127.own_ref = bf16[40,2048]{1,0:T(8,128)(2,1)} custom-call(f32[40,4160]{1,0:T(8,128)S(1)} %copy-done.4, f32[1,128]{1,0:T(1,128)S(1)} %pad_bitcast_fusion.taps_ref, s32[1,40]{1,0:T(1,128)S(1)} %bitcast.16, bf16[256,2048]{1,0:T(8,128)(2,1)S(1)} %copy-done.3, bf16[256,2048]{1,0:T(8,128)(2,1)S(1)} %copy-done.2, f32[8,1024]{1,0:T(8,128)S(1)} %copy-done.7, ...), custom_call_target="tpu_custom_call" | custom-call | tf_op jit(solution)/shard_map/pallas_call | solution.py:148
  17.0 0.0 all-gather.5.cloned.1.call-update
  17.0 0.0 all-gather.7.cloned.1.call-start
  17.1 0.0 copy-done.10
  17.1 0.6 fusion.1
  21.2 33.3 %all-gather.5.cloned.1.call-done = bf16[640,2048]{1,0:T(8,128)(2,1)} async-done(((bf16[40,2048]{1,0:T(8,128)(2,1)}), bf16[640,2048]{1,0:T(8,128)(2,1)}) %all-gather.5.cloned.1.call-update) | async-done | bytes 2621456 | tf_op jit(solution)/shard_map/all_gather | solution.py:183
  54.5 1.0 constant_dynamic-slice_fusion.1
  55.5 0.8 pad_maximum_fusion
  56.3 0.0 all-gather.7.cloned.1.call-update
  56.3 0.0 copy-done.11
  56.3 0.6 fusion
  60.4 55.1 %all-gather.7.cloned.1.call-done = bf16[16,40,2048]{2,1,0:T(8,128)(2,1)} async-done(((bf16[2,40,2048]{2,1,0:T(8,128)(2,1)}), bf16[16,40,2048]{2,1,0:T(8,128)(2,1)}) %all-gather.7.cloned.1.call-update) | async-done | bytes 2621456 | tf_op jit(solution)/shard_map/all_gather | solution.py:187
  115.5 1.0 dynamic-slice_bitcast_fusion.1
  116.5 0.0 copy-done
  116.6 0.0 copy-done.5
  116.6 0.0 copy-done.8
  116.6 0.0 copy-start.1
  116.6 1.6 %copy-done.1 = bf16[1024,1024]{1,0:T(8,128)(2,1)S(1)} copy-done((bf16[1024,1024]{1,0:T(8,128)(2,1)S(1)}, bf16[1024,1024]{1,0:T(8,128)(2,1)}, u32[]{:S(2)}) %copy-start.1) | copy-done | bytes 2097176
  118.2 23.0 %shard_map.128 = bf16[3200,2048]{1,0:T(8,128)(2,1)} custom-call(bf16[40,2048]{1,0:T(8,128)(2,1)} %shard_map.127.own_ref, bf16[2,40,2048]{2,1,0:T(8,128)(2,1)S(1)} %pad_maximum_fusion.1.their_ref, bf16[1024,1024]{1,0:T(8,128)(2,1)S(1)} %copy-done.1, bf16[1024,1024]{1,0:T(8,128)(2,1)S(1)} %copy-done, f32[2,1024]{1,0:T(2,128)S(1)} %copy-done.8, ...), custom_call_target="tpu_custom_call" | custom-call | tf_op jit(solution)/shard_map/pallas_call | solution.py:163
  (1 shorter events, 0.0 us)
Async XLA Ops:
  6.5 10.6 %copy-start.10 = (s32[2,1,1]{0,2,1:T(1,128)S(1)}, s32[2,1,1]{0,2,1:T(1,128)}, u32[]{:S(2)}) copy-start(s32[2,1,1]{0,2,1:T(1,128)} %param.17) | copy-start | bytes 28
  6.5 49.8 %copy-start.11 = (s32[2,1]{0,1:T(1,128)S(1)}, s32[2,1]{0,1:T(1,128)}, u32[]{:S(2)}) copy-start(s32[2,1]{0,1:T(1,128)} %param.16) | copy-start | bytes 28
  6.5 48.0 %all-gather.5.cloned.1.call-start = ((), (), s32[]{:S(2)}) async-start(), calls=%async_computation | async-start | bytes 2785280 | tf_op jit(solution)/shard_map/all_gather | solution.py:183
  7.2 1.2 copy-start.2
  8.4 1.2 copy-start.3
  9.7 1.1 copy-start.4
  10.8 0.8 copy-start.6
  11.5 0.8 copy-start.7
  12.3 0.7 copy-start.9
  12.9 103.6 %copy-start = (bf16[1024,1024]{1,0:T(8,128)(2,1)S(1)}, bf16[1024,1024]{1,0:T(8,128)(2,1)}, u32[]{:S(2)}) copy-start(bf16[1024,1024]{1,0:T(8,128)(2,1)} %constant.39.clone.sin_ref) | copy-start | bytes 6291460
  12.9 103.6 %copy-start.5 = (bf16[256,256]{1,0:T(8,128)(2,1)S(1)}, bf16[256,256]{1,0:T(8,128)(2,1)}, u32[]{:S(2)}) copy-start(bf16[256,256]{1,0:T(8,128)(2,1)} %constant.41.clone.flip_ref) | copy-start | bytes 393220
  12.9 103.6 %copy-start.8 = (f32[2,1024]{1,0:T(2,128)S(1)}, f32[2,1024]{1,0:T(2,128)}, u32[]{:S(2)}) copy-start(f32[2,1024]{1,0:T(2,128)} %constant.40.clone.turn_ref) | copy-start | bytes 24580
  17.0 98.4 %all-gather.7.cloned.1.call-start = ((), (), s32[]{:S(2)}) async-start(), calls=%async_computation.1 | async-start | bytes 2949120 | tf_op jit(solution)/shard_map/all_gather | solution.py:187
  116.6 1.6 %copy-start.1 = (bf16[1024,1024]{1,0:T(8,128)(2,1)S(1)}, bf16[1024,1024]{1,0:T(8,128)(2,1)}, u32[]{:S(2)}) copy-start(bf16[1024,1024]{1,0:T(8,128)(2,1)} %constant.38.clone.cos_ref) | copy-start | bytes 6291460
Sparse Core Ops, SparseCore 0:
  17.2 37.2 all-gather.4
  56.8 58.6 all-gather.6
where the time goes:
time: 149 us; the launch traced here: 148 us
  waiting for transfers between devices  88.4 us (59%)
  Pallas kernels  27.1 us (18%)
  between operations  20.5 us (14%)
  local copies, waits for them, and re-layouts  11.2 us (8%)
    all_gather x1, waiting for transfers between devices, per_device(): around = lax.all_gather(picked, 'group', axis=0)  55.1 us
    all_gather x1, waiting for transfers between devices, per_device(): mine = lax.all_gather(panel, 'member', axis=0)  33.3 us
    pallas_call x1, Pallas kernels, correlate(): pl.pallas_call(correlate_kernel, grid=(ROUNDS, steps), out_shape=jax.Shap...  23 us
    unnamed x24, local copies, waits for them, and re-layouts  7.32 us
    pallas_call x1, Pallas kernels, whiten(): pl.pallas_call(whiten_kernel, out_shape=jax.ShapeDtypeStruct((CH, 2 * NBI...  4.06 us
  transfers between devices with their start and end apart: 2, of which 2 were waited for; matrix products, arithmetic and copies ran while one was open for 1% of the time, Pallas kernels for 0%

commit v1 on v0

--- a/solution.py
+++ b/solution.py
@@ -111,18 +111,32 @@
     total = jnp.where(col > final, total[:, final : final + 1], total)
     inverse = lax.rsqrt(total * (1.0 / WIN) + EPS)
     place = (lax.broadcasted_iota(jnp.int32, (CH, CH), 0) == slot_ref[...]).astype(F32).astype(BF16)
-    panel_ref[:, :NBIN] = dot(place, (re * inverse).astype(BF16)).astype(BF16)
-    panel_ref[:, NBIN:] = dot(place, (im * inverse).astype(BF16)).astype(BF16)
-
-
-def correlate_kernel(own_ref, their_ref, cos_ref, sin_ref, turn_ref, flip_ref, out_ref, cre_ref, cim_ref):
-    br = their_ref[0, :, :NBIN].astype(F32)
-    bi = their_ref[0, :, NBIN:].astype(F32)
-    tr, ti = turn_ref[0:1, :], turn_ref[1:2, :]
-    own = own_ref[...].astype(F32)
-    ar0, ai0 = own[:, :NBIN], own[:, NBIN:]
-    ar = ar0 * tr - ai0 * ti
-    ai = ar0 * ti + ai0 * tr
+    re = dot(place, (re * inverse).astype(BF16))
+    im = dot(place, (im * inverse).astype(BF16))
+    for n in range(2):
+        cols = slice(HALF * n, HALF * (n + 1))
+        panel_ref[n] = jnp.concatenate([re[:, cols], im[:, cols]], axis=0).astype(BF16)
+
+
+def whole_bins(panel):
+    wide = panel.astype(F32)
+    return (
+        jnp.concatenate([wide[0, :CH], wide[1, :CH]], axis=1),
+        jnp.concatenate([wide[0, CH:], wide[1, CH:]], axis=1),
+    )
+
+
+def correlate_kernel(own_ref, their_ref, cos_ref, sin_ref, turn_ref, flip_ref, out_ref, turned_ref, cre_ref, cim_ref):
+    @pl.when((pl.program_id(0) == 0) & (pl.program_id(1) == 0))
+    def _():
+        own_re, own_im = whole_bins(own_ref[...])
+        tr, ti = turn_ref[0:1, :], turn_ref[1:2, :]
+        turned_ref[0] = own_re * tr - own_im * ti
+        turned_ref[1] = own_re * ti + own_im * tr
+
+    br, bi = whole_bins(their_ref[0])
+    at = pl.ds(pl.multiple_of(pl.program_id(1) * OWN_STEP, OWN_STEP), OWN_STEP)
+    ar, ai = turned_ref[0, at, :], turned_ref[1, at, :]
     for i in range(0, OWN_STEP, 2):
         res, ims = [], []
         for k in (i, i + 1):
@@ -142,12 +156,165 @@
         out_ref[:, LAG - width * (n + 1) : LAG - width * n] = mirrored.astype(BF16)
 
 
+HALF = NBIN // 2
+MESH_ID = pl.DeviceIdType.MESH
+
+
+def choose(first, a, b):
+    return jnp.where(first, a.astype(F32), b.astype(F32)).astype(BF16)
+
+
+def exchange_kernel(pairings_ref, subset_ref, panel_ref, theirs_ref, meta, peers, flat, row, rows0, rows1, line, lines0, lines1,
+                    row_in, rows_in, line_in, lines_in, row_out, rows_out, line_out, lines_out, send, recv, local):
+    g, m = lax.axis_index("group"), lax.axis_index("member")
+    z, h = g // 2, g % 2
+    l, x, c = m // 8, (m // 2) % 4, m % 2
+    k = x * 2 + c
+
+    def at(dz=0, dh=0, dl=0, dx=0, dc=0):
+        group = lax.rem(z + dz, 4) * 2 + lax.rem(h + dh, 2)
+        member = lax.rem(l + dl, 2) * 8 + lax.rem(x + dx, 4) * 2 + lax.rem(c + dc, 2)
+        return group, member
+
+    along_x = [at(dx=d) for d in (1, 3, 2)]
+    along_z = [at(dz=d) for d in (1, 3, 2)]
+    core, low, high = at(dc=1), at(dl=1), at(dh=1)
+    started = []
+
+    def put(src, dst, where):
+        n = len(started)
+        copy = pltpu.make_async_remote_copy(
+            src_ref=src, dst_ref=dst, send_sem=send.at[n], recv_sem=recv.at[n], device_id=where, device_id_type=MESH_ID
+        )
+        copy.start()
+        started.append(copy)
+        return copy
+
+    index = lax.broadcasted_iota(jnp.int32, (8, 128), 0)
+    mine = jnp.zeros((8, 128), jnp.int32)
+    for r in range(ROUNDS):
+        mine = jnp.where(index == r, pairings_ref[r, 0], mine)
+        mine = jnp.where(index == ROUNDS + r, subset_ref[r, 0], mine)
+    meta[...] = mine
+
+    barrier = pltpu.get_barrier_semaphore()
+    everyone = along_x + along_z + [core, low, high]
+    for where in everyone:
+        pl.semaphore_signal(barrier, inc=1, device_id=where, device_id_type=MESH_ID)
+    pl.semaphore_wait(barrier, len(everyone))
+
+    asks = [put(meta, peers.at[0], low), put(meta, peers.at[1], high)]
+    row[k] = panel_ref[0]
+    line[z] = panel_ref[1]
+    row_x = [put(panel_ref.at[0], row.at[k], where) for where in along_x]
+    line_z = [put(panel_ref.at[1], line.at[z], where) for where in along_z]
+    row_c = [put(panel_ref.at[0], row.at[k], core)]
+    for ask in asks:
+        ask.wait_recv()
+    fetch = pltpu.make_async_copy(peers, flat, local)
+    fetch.start()
+    fetch.wait()
+    my_pair = [pairings_ref[r, 0] for r in range(ROUNDS)]
+    my_sub = [subset_ref[r, 0] for r in range(ROUNDS)]
+    low_sub = [flat[0, ROUNDS + r, 0] for r in range(ROUNDS)]
+    high_pair = [flat[1, r, 0] for r in range(ROUNDS)]
+
+    def slot(dx):
+        return lax.rem(x + dx, 4) * 2 + c
+
+    for copy, dx in zip(row_x, (3, 1, 2)):
+        copy.wait_recv()
+        row_c.append(put(row.at[slot(dx)], row.at[slot(dx)], core))
+    for copy in line_z:
+        copy.wait_recv()
+    rows, lines = (rows0, rows1), (lines0, lines1)
+    in_group = [lax.rem(my_pair[r], 2) == h for r in range(ROUNDS)]
+    in_member = [my_sub[r] // 8 == l for r in range(ROUNDS)]
+    my_z = [my_pair[r] // 2 for r in range(ROUNDS)]
+    my_k = [lax.rem(my_sub[r], 8) for r in range(ROUNDS)]
+    line_y = []
+    for r in range(ROUNDS):
+        line_out[r] = line[high_pair[r] // 2]
+        line_y.append(put(line_out.at[r], line_in.at[r], high))
+    for copy in row_c:
+        copy.wait_recv()
+    row_y = []
+    for r in range(ROUNDS):
+        row_out[r] = row[lax.rem(low_sub[r], 8)]
+        row_y.append(put(row_out.at[r], row_in.at[r], low))
+
+    rows_x, rows_c, lines_z = [], [], []
+    for r in range(ROUNDS):
+        line_y[r].wait_recv()
+        rows[r][k] = choose(in_group[r], line[my_z[r]], line_in[r])
+        own = rows[r].at[k]
+        rows_x.append([put(own, own, where) for where in along_x])
+        rows_c.append([put(own, own, core)])
+        row_y[r].wait_recv()
+        lines[r][z] = choose(in_member[r], row[my_k[r]], row_in[r])
+        own = lines[r].at[z]
+        lines_z.append([put(own, own, where) for where in along_z])
+    last_line, last_row = [], []
+    for r in range(ROUNDS):
+        for copy, dx in zip(rows_x[r], (3, 1, 2)):
+            copy.wait_recv()
+            got = rows[r].at[slot(dx)]
+            rows_c[r].append(put(got, got, core))
+        for copy in lines_z[r]:
+            copy.wait_recv()
+        lines_out[r] = lines[r][high_pair[r] // 2]
+        last_line.append(put(lines_out.at[r], lines_in.at[r], high))
+        for copy in rows_c[r]:
+            copy.wait_recv()
+        rows_out[r] = rows[r][lax.rem(low_sub[r], 8)]
+        last_row.append(put(rows_out.at[r], rows_in.at[r], low))
+    for r in range(ROUNDS):
+        last_line[r].wait_recv()
+        theirs_ref[r, 0] = choose(in_group[r], lines[r][my_z[r]], lines_in[r])
+        last_row[r].wait_recv()
+        theirs_ref[r, 1] = choose(in_member[r], rows[r][my_k[r]], rows_in[r])
+    for copy in started:
+        copy.wait_send()
+
+
+COPIES = 2 + 7 + 3 + 2 + 2 + 14 + 6 + 2 + 2
+
+
+def exchange(panel, pairings, subset):
+    half = (2 * CH, HALF)
+    return pl.pallas_call(
+        exchange_kernel,
+        out_shape=jax.ShapeDtypeStruct((ROUNDS, 2) + half, BF16),
+        in_specs=[pl.BlockSpec(memory_space=pltpu.SMEM)] * 2 + [pl.BlockSpec(memory_space=pltpu.VMEM)],
+        out_specs=pl.BlockSpec(memory_space=pltpu.VMEM),
+        scratch_shapes=[
+            pltpu.VMEM((8, 128), jnp.int32),
+            pltpu.VMEM((2, 8, 128), jnp.int32),
+            pltpu.SMEM((2, 8, 128), jnp.int32),
+            pltpu.VMEM((8,) + half, BF16),
+            pltpu.VMEM((8,) + half, BF16),
+            pltpu.VMEM((8,) + half, BF16),
+            pltpu.VMEM((4,) + half, BF16),
+            pltpu.VMEM((4,) + half, BF16),
+            pltpu.VMEM((4,) + half, BF16),
+        ]
+        + [pltpu.VMEM((ROUNDS,) + half, BF16)] * 8
+        + [
+            pltpu.SemaphoreType.DMA((COPIES,)),
+            pltpu.SemaphoreType.DMA((COPIES,)),
+            pltpu.SemaphoreType.DMA,
+        ],
+        compiler_params=pltpu.CompilerParams(collective_id=1, has_side_effects=True, vmem_limit_bytes=16 * MIB),
+        name="exchange",
+    )(pairings, subset, panel)
+
+
 def whiten(raw_strain, fir_taps, block_slot):
     high, low, tc, ts = forward_tables()
     taps = jnp.pad(fir_taps, (0, 128 - TAPS)).reshape(1, 128)
     return pl.pallas_call(
         whiten_kernel,
-        out_shape=jax.ShapeDtypeStruct((CH, 2 * NBIN), BF16),
+        out_shape=jax.ShapeDtypeStruct((2, 2 * CH, HALF), BF16),
         in_specs=[pl.BlockSpec(memory_space=pltpu.VMEM)] * 7,
         out_specs=pl.BlockSpec(memory_space=pltpu.VMEM),
         scratch_shapes=[pltpu.VMEM((PIECES * CH, PIECE), BF16)] * 2 + [pltpu.VMEM((CH, NBIN), F32)] * 2,
@@ -165,29 +332,22 @@
         grid=(ROUNDS, steps),
         out_shape=jax.ShapeDtypeStruct((ROUNDS * CH * CH, 2 * LAG), BF16),
         in_specs=[
-            pl.BlockSpec((OWN_STEP, 2 * NBIN), lambda r, i: (i, 0)),
-            pl.BlockSpec((1, CH, 2 * NBIN), lambda r, i: (r, 0, 0)),
+            pl.BlockSpec((2, 2 * CH, HALF), lambda r, i: (0, 0, 0)),
+            pl.BlockSpec((1, 2, 2 * CH, HALF), lambda r, i: (r, 0, 0, 0)),
             pl.BlockSpec((NBIN, LAG), whole),
             pl.BlockSpec((NBIN, LAG), whole),
             pl.BlockSpec((2, NBIN), whole),
             pl.BlockSpec((256, 256), whole),
         ],
         out_specs=pl.BlockSpec((rows, 2 * LAG), lambda r, i: (r * steps + i, 0)),
-        scratch_shapes=[pltpu.VMEM((rows, NBIN), BF16)] * 2,
+        scratch_shapes=[pltpu.VMEM((2, CH, NBIN), F32)] + [pltpu.VMEM((rows, NBIN), BF16)] * 2,
         compiler_params=pltpu.CompilerParams(vmem_limit_bytes=48 * MIB),
     )(own, theirs, cosine, sine, turn, flip)
 
 
 def per_device(raw_strain, fir_taps, block_slot, pairings, pair_subset):
     panel = whiten(raw_strain, fir_taps, block_slot)
-    mine = lax.all_gather(panel, "member", axis=0)
-    picked = jnp.stack(
-        [lax.dynamic_index_in_dim(mine, pair_subset[r, 0, 0], 0, keepdims=False) for r in range(ROUNDS)]
-    )
-    around = lax.all_gather(picked, "group", axis=0)
-    theirs = jnp.stack(
-        [lax.dynamic_index_in_dim(around, pairings[r, 0], 0, keepdims=False)[r] for r in range(ROUNDS)]
-    )
+    theirs = exchange(panel, pairings, pair_subset.reshape(ROUNDS, 1))
     result = correlate(panel, theirs)
     return result.reshape(ROUNDS, KSUB, CH, CH, 2 * LAG)
 

time: 149 us -> 69.5 us (0.47)
  waiting for transfers between devices: 88.4 us -> 0 us
  Pallas kernels: 27.1 us -> 59.4 us
  between operations: 20.5 us -> 0.06 us
  local copies, waits for them, and re-layouts: 11.2 us -> 9.6 us
    all_gather x2 -> x0, waiting for transfers between devices: 88.4 us -> none  [the longest x1 55.1 us: per_device(): around = lax.all_gather(picked, 'group', axis=0)]
    pallas_call x1 -> x2, Pallas kernels: 4.06 us -> 37.5 us  [the longest x1 34.1 us: exchange(): pl.pallas_call(exchange_kernel, out_shape=jax.ShapeDtypeStruct((ROUNDS, 2...]
    slice x3 -> x0, local copies, waits for them, and re-layouts: 2.16 us -> none  [the longest x1 1.02 us: per_device(): lax.dynamic_index_in_dim(around, pairings[r, 0], 0, keepdims=False)[r]]
    unnamed x24 -> x21, local copies, waits for them, and re-layouts: 7.32 us -> 8.05 us
  transfers between devices with their start and end apart: 2 -> 0, of which waited for: 2 -> 0; matrix products, arithmetic and copies ran while one was open for 1% -> 0% of each run, Pallas kernels for 0% -> 0%
where the time goes in v1:
time: 69.5 us; the launch traced here: 69.1 us
  Pallas kernels  59.4 us (85%)
  local copies, waits for them, and re-layouts  9.6 us (14%)
    pallas_call x1, Pallas kernels, exchange(): pl.pallas_call(exchange_kernel, out_shape=jax.ShapeDtypeStruct((ROUNDS, 2...  34.1 us
    pallas_call x1, Pallas kernels, correlate(): pl.pallas_call(correlate_kernel, grid=(ROUNDS, steps), out_shape=jax.Shap...  21.9 us
    unnamed x21, local copies, waits for them, and re-layouts  8.05 us
    pallas_call x1, Pallas kernels, whiten(): pl.pallas_call(whiten_kernel, out_shape=jax.ShapeDtypeStruct((2, 2 * CH,...  3.4 us

profile of v1, /device:TPU:0, one launch (start us, length us, event | category | flops | bytes accessed | tf_op | source)
XLA Modules:
  0.0 69.1 jit_solution(12470054023803825970)
XLA Ops:
  0.0 0.0 copy-start
  0.0 0.8 %pad_bitcast_fusion.taps_ref = f32[1,128]{1,0:T(1,128)S(1)} fusion(f32[64]{0:T(128)} %param.14), kind=kLoop, calls=%fused_computation | loop fusion | bytes 768 | tf_op jit(solution)/shard_map/reshape | solution.py:314
  0.8 0.7 %copy.14.pairings_ref = s32[2,1]{1,0:T(2,128)S(1)} copy(s32[2,1]{0,1:T(1,128)} %param.16) | data formatting | bytes 16 | tf_op args[3]
  1.6 0.7 %copy.15.subset_ref = s32[2,1]{1,0:T(2,128)S(1)} copy(s32[2,1]{0,1:T(1,128)} %bitcast.8) | data formatting | bytes 16 | tf_op jit(solution)/shard_map/reshape | solution.py:350
  2.3 0.0 copy-start.2
  2.3 1.2 %copy-done.2 = bf16[256,2048]{1,0:T(8,128)(2,1)S(1)} copy-done((bf16[256,2048]{1,0:T(8,128)(2,1)S(1)}, bf16[256,2048]{1,0:T(8,128)(2,1)}, u32[]{:S(2)}) %copy-start.2) | copy-done | bytes 1048600
  3.5 0.0 copy-start.3
  3.5 1.2 %copy-done.3 = bf16[256,2048]{1,0:T(8,128)(2,1)S(1)} copy-done((bf16[256,2048]{1,0:T(8,128)(2,1)S(1)}, bf16[256,2048]{1,0:T(8,128)(2,1)}, u32[]{:S(2)}) %copy-start.3) | copy-done | bytes 1048600
  4.7 0.0 copy-start.4
  4.7 1.1 %copy-done.4 = f32[40,4160]{1,0:T(8,128)S(1)} copy-done((f32[40,4160]{1,0:T(8,128)S(1)}, f32[40,4160]{1,0:T(8,128)}, u32[]{:S(2)}) %copy-start.4) | copy-done | bytes 665624
  5.8 0.0 copy-start.6
  5.8 0.8 %copy-done.6 = f32[8,1024]{1,0:T(8,128)S(1)} copy-done((f32[8,1024]{1,0:T(8,128)S(1)}, f32[8,1024]{1,0:T(8,128)}, u32[]{:S(2)}) %copy-start.6) | copy-done | bytes 32792
  6.6 0.0 copy-start.7
  6.6 0.8 %copy-done.7 = f32[8,1024]{1,0:T(8,128)S(1)} copy-done((f32[8,1024]{1,0:T(8,128)S(1)}, f32[8,1024]{1,0:T(8,128)}, u32[]{:S(2)}) %copy-start.7) | copy-done | bytes 32792
  7.4 0.0 copy-start.9
  7.4 0.7 copy-done.9
  8.0 0.0 copy-start.5
  8.0 0.0 copy-start.8
  8.0 3.4 %shard_map.127.panel_ref.own_ref = bf16[2,80,512]{2,1,0:T(8,128)(2,1)S(1)} custom-call(f32[40,4160]{1,0:T(8,128)S(1)} %copy-done.4, f32[1,128]{1,0:T(1,128)S(1)} %pad_bitcast_fusion.taps_ref, s32[1,40]{1,0:T(1,128)S(1)} %bitcast.7, bf16[256,2048]{1,0:T(8,128)(2,1)S(1)} %copy-done.3, bf16[256,2048]{1,0:T(8,128)(2,1)S(1)} %copy-done.2, ...), custom_call_target="tpu_custom_call" | custom-call | tf_op jit(solution)/shard_map/pallas_call | solution.py:315
  11.4 34.1 %exchange.1.their_ref = bf16[2,2,80,512]{3,2,1,0:T(8,128)(2,1)S(1)} custom-call(s32[2,1]{1,0:T(2,128)S(1)} %copy.14.pairings_ref, s32[2,1]{1,0:T(2,128)S(1)} %copy.15.subset_ref, bf16[2,80,512]{2,1,0:T(8,128)(2,1)S(1)} %shard_map.127.panel_ref.own_ref), custom_call_target="tpu_custom_call" | custom-call | tf_op jit(solution)/shard_map/exchange/pallas_call | solution.py:285
  45.5 0.0 copy-done
  45.6 0.0 copy-done.5
  45.6 0.0 copy-done.8
  45.6 0.0 copy-start.1
  45.6 1.6 %copy-done.1 = bf16[1024,1024]{1,0:T(8,128)(2,1)S(1)} copy-done((bf16[1024,1024]{1,0:T(8,128)(2,1)S(1)}, bf16[1024,1024]{1,0:T(8,128)(2,1)}, u32[]{:S(2)}) %copy-start.1) | copy-done | bytes 2097176
  47.2 21.9 %shard_map.128 = bf16[3200,2048]{1,0:T(8,128)(2,1)} custom-call(bf16[2,80,512]{2,1,0:T(8,128)(2,1)S(1)} %shard_map.127.panel_ref.own_ref, bf16[2,2,80,512]{3,2,1,0:T(8,128)(2,1)S(1)} %exchange.1.their_ref, bf16[1024,1024]{1,0:T(8,128)(2,1)S(1)} %copy-done.1, bf16[1024,1024]{1,0:T(8,128)(2,1)S(1)} %copy-done, f32[2,1024]{1,0:T(2,128)S(1)} %copy-done.8, ...), custom_call_target="tpu_custom_call" | custom-call | tf_op jit(solution)/shard_map/pallas_call | solution.py:330
Async XLA Ops:
  0.0 45.5 %copy-start = (bf16[1024,1024]{1,0:T(8,128)(2,1)S(1)}, bf16[1024,1024]{1,0:T(8,128)(2,1)}, u32[]{:S(2)}) copy-start(bf16[1024,1024]{1,0:T(8,128)(2,1)} %constant.24.clone.sin_ref) | copy-start | bytes 6291460
  2.3 1.2 %copy-start.2 = (bf16[256,2048]{1,0:T(8,128)(2,1)S(1)}, bf16[256,2048]{1,0:T(8,128)(2,1)}, u32[]{:S(2)}) copy-start(bf16[256,2048]{1,0:T(8,128)(2,1)} %constant.20.clone.low_ref) | copy-start | bytes 3145732
  3.5 1.2 %copy-start.3 = (bf16[256,2048]{1,0:T(8,128)(2,1)S(1)}, bf16[256,2048]{1,0:T(8,128)(2,1)}, u32[]{:S(2)}) copy-start(bf16[256,2048]{1,0:T(8,128)(2,1)} %constant.19.clone.high_ref) | copy-start | bytes 3145732
  4.7 1.1 %copy-start.4 = (f32[40,4160]{1,0:T(8,128)S(1)}, f32[40,4160]{1,0:T(8,128)}, u32[]{:S(2)}) copy-start(f32[40,4160]{1,0:T(8,128)} %raw_ref.1) | copy-start | bytes 1996804
  5.8 0.8 %copy-start.6 = (f32[8,1024]{1,0:T(8,128)S(1)}, f32[8,1024]{1,0:T(8,128)}, u32[]{:S(2)}) copy-start(f32[8,1024]{1,0:T(8,128)} %constant.22.clone.ts_ref) | copy-start | bytes 98308
  6.6 0.8 %copy-start.7 = (f32[8,1024]{1,0:T(8,128)S(1)}, f32[8,1024]{1,0:T(8,128)}, u32[]{:S(2)}) copy-start(f32[8,1024]{1,0:T(8,128)} %constant.21.clone.tc_ref) | copy-start | bytes 98308
  7.4 0.7 copy-start.9
  8.0 37.5 %copy-start.5 = (bf16[256,256]{1,0:T(8,128)(2,1)S(1)}, bf16[256,256]{1,0:T(8,128)(2,1)}, u32[]{:S(2)}) copy-start(bf16[256,256]{1,0:T(8,128)(2,1)} %constant.26.clone.flip_ref) | copy-start | bytes 393220
  8.0 37.6 %copy-start.8 = (f32[2,1024]{1,0:T(2,128)S(1)}, f32[2,1024]{1,0:T(2,128)}, u32[]{:S(2)}) copy-start(f32[2,1024]{1,0:T(2,128)} %constant.25.clone.turn_ref) | copy-start | bytes 24580
  45.6 1.6 %copy-start.1 = (bf16[1024,1024]{1,0:T(8,128)(2,1)S(1)}, bf16[1024,1024]{1,0:T(8,128)(2,1)}, u32[]{:S(2)}) copy-start(bf16[1024,1024]{1,0:T(8,128)(2,1)} %constant.23.clone.cos_ref) | copy-start | bytes 6291460

commit v2 on v1

--- a/solution.py
+++ b/solution.py
@@ -28,6 +28,7 @@
 SPAN = 640
 OWN_STEP = 8
 MIB = 1 << 20
+GRANT = 63 * MIB
 BF16 = jnp.bfloat16
 F32 = jnp.float32
 
@@ -43,7 +44,7 @@
     phases = np.arange(PIECE)[:, None] * bins[None, :] % NFFT * (2.0 * math.pi / NFFT)
     high, low = split_bf16(np.concatenate([np.cos(phases), -np.sin(phases)], axis=1))
     shift = np.arange(PIECES)[:, None] * PIECE * bins[None, :] % NFFT * (2.0 * math.pi / NFFT)
-    return high, low, np.cos(shift).astype(np.float32), -np.sin(shift).astype(np.float32)
+    return np.stack([high, low]), np.stack([np.cos(shift), -np.sin(shift)]).astype(np.float32)
 
 
 def lag_tables():
@@ -54,8 +55,7 @@
     sine = (-np.sin(phases) * scale).astype(ml_dtypes.bfloat16)
     half = bins * (math.pi / NFFT)
     turn = np.stack([np.cos(half), -np.sin(half)]).astype(np.float32)
-    flip = np.eye(256)[::-1].astype(ml_dtypes.bfloat16)
-    return cosine, sine, turn, flip
+    return np.stack([cosine, sine]), turn
 
 
 def dot(a, b):
@@ -67,9 +67,12 @@
     return high, (x - high.astype(F32)).astype(BF16)
 
 
-def whiten_kernel(raw_ref, taps_ref, slot_ref, high_ref, low_ref, tc_ref, ts_ref, panel_ref, dh_ref, dl_ref, re_ref, im_ref):
-    taps = jnp.concatenate([taps_ref[...], jnp.zeros((1, SPAN - 128), F32)], axis=1)
-    filter_rows = pltpu.roll(jnp.broadcast_to(taps, (PIECE, SPAN)), 0, 1, stride=2, stride_axis=0)
+def whiten_block(raw_ref, taps_ref, slot_ref, tables_ref, shift_ref, panel_ref, filter_ref, dh_ref, dl_ref, re_ref, im_ref, loads):
+    for load in loads[:3]:
+        load.wait()
+    filter_ref[...] = jnp.zeros((1, SPAN), F32)
+    filter_ref[:, :TAPS] = taps_ref[...]
+    filter_rows = pltpu.roll(jnp.broadcast_to(filter_ref[...], (PIECE, SPAN)), 0, 1, stride=2, stride_axis=0)
     pieces = [raw_ref[:, 2 * PIECE * b : 2 * PIECE * b + SPAN] for b in range(PIECES - 1)]
     last = raw_ref[:, 2 * PIECE * (PIECES - 1) :]
     pieces.append(jnp.concatenate([last, jnp.zeros((CH, SPAN - last.shape[1]), F32)], axis=1))
@@ -81,6 +84,8 @@
     dh, dl = parts(contract(xh, fh) + contract(xl, fh) + contract(xh, fl))
     dh_ref[...] = dh
     dl_ref[...] = dl
+    for load in loads[3:]:
+        load.wait()
     width = 256
     for n in range(NBIN // width):
         cols = slice(width * n, width * (n + 1))
@@ -88,13 +93,15 @@
         for base in (0, NBIN):
             at = slice(base + width * n, base + width * (n + 1))
             wide = dh_ref[...]
-            both.append(dot(wide, high_ref[:, at]) + dot(dl_ref[...], high_ref[:, at]) + dot(wide, low_ref[:, at]))
+            both.append(
+                dot(wide, tables_ref[0, :, at]) + dot(dl_ref[...], tables_ref[0, :, at]) + dot(wide, tables_ref[1, :, at])
+            )
         yr, yi = both
         re = jnp.zeros((CH, width), F32)
         im = jnp.zeros((CH, width), F32)
         for b in range(PIECES):
-            tc = tc_ref[b : b + 1, cols]
-            ts = ts_ref[b : b + 1, cols]
+            tc = shift_ref[0, b : b + 1, cols]
+            ts = shift_ref[1, b : b + 1, cols]
             r, i = yr[CH * b : CH * (b + 1)], yi[CH * b : CH * (b + 1)]
             re += r * tc - i * ts
             im += r * ts + i * tc
@@ -126,13 +133,20 @@
     )
 
 
-def correlate_kernel(own_ref, their_ref, cos_ref, sin_ref, turn_ref, flip_ref, out_ref, turned_ref, cre_ref, cim_ref):
-    @pl.when((pl.program_id(0) == 0) & (pl.program_id(1) == 0))
+def correlate_kernel(own_ref, their_ref, lag_hbm, turn_ref, out_ref, lag_ref, turned_ref, cre_ref, cim_ref, load_sem):
+    first = (pl.program_id(0) == 0) & (pl.program_id(1) == 0)
+    loads = [pltpu.make_async_copy(lag_hbm.at[n], lag_ref.at[n], load_sem.at[n]) for n in range(2)]
+
+    @pl.when(first)
     def _():
+        for load in loads:
+            load.start()
         own_re, own_im = whole_bins(own_ref[...])
         tr, ti = turn_ref[0:1, :], turn_ref[1:2, :]
         turned_ref[0] = own_re * tr - own_im * ti
         turned_ref[1] = own_re * ti + own_im * tr
+        for load in loads:
+            load.wait()
 
     br, bi = whole_bins(their_ref[0])
     at = pl.ds(pl.multiple_of(pl.program_id(1) * OWN_STEP, OWN_STEP), OWN_STEP)
@@ -146,14 +160,18 @@
         rows = slice(CH * i, CH * (i + 2))
         cre_ref[rows, :] = jnp.concatenate(res, axis=0).astype(BF16)
         cim_ref[rows, :] = jnp.concatenate(ims, axis=0).astype(BF16)
-    width = 256
+    backwards = 127 - lax.broadcasted_iota(jnp.int32, (OWN_STEP * CH, 128), 1)
+    width = 512
     for n in range(LAG // width):
         cols = slice(width * n, width * (n + 1))
-        even = dot(cre_ref[...], cos_ref[:, cols])
-        odd = dot(cim_ref[...], sin_ref[:, cols])
+        even = dot(cre_ref[...], lag_ref[0, :, cols])
+        odd = dot(cim_ref[...], lag_ref[1, :, cols])
         out_ref[:, LAG + width * n : LAG + width * (n + 1)] = (even + odd).astype(BF16)
-        mirrored = dot((even - odd).astype(BF16), flip_ref[...])
-        out_ref[:, LAG - width * (n + 1) : LAG - width * n] = mirrored.astype(BF16)
+        for q in range(width // 128):
+            piece = even[:, 128 * q : 128 * (q + 1)] - odd[:, 128 * q : 128 * (q + 1)]
+            piece = jnp.take_along_axis(piece, backwards, axis=1, mode="promise_in_bounds")
+            low = LAG - width * n - 128 * (q + 1)
+            out_ref[:, low : low + 128] = piece.astype(BF16)
 
 
 HALF = NBIN // 2
@@ -164,7 +182,9 @@
     return jnp.where(first, a.astype(F32), b.astype(F32)).astype(BF16)
 
 
-def exchange_kernel(pairings_ref, subset_ref, panel_ref, theirs_ref, meta, peers, flat, row, rows0, rows1, line, lines0, lines1,
+def exchange_kernel(pairings_ref, subset_ref, raw_hbm, taps_hbm, slot_hbm, tables_hbm, shift_hbm, panel_ref, theirs_ref,
+                    raw_ref, taps_ref, slot_ref, tables_ref, shift_ref, filter_ref, dh_ref, dl_ref, re_ref, im_ref, load_sem,
+                    meta, peers, flat, row, rows0, rows1, line, lines0, lines1,
                     row_in, rows_in, line_in, lines_in, row_out, rows_out, line_out, lines_out, send, recv, local):
     g, m = lax.axis_index("group"), lax.axis_index("member")
     z, h = g // 2, g % 2
@@ -190,17 +210,25 @@
         started.append(copy)
         return copy
 
-    index = lax.broadcasted_iota(jnp.int32, (8, 128), 0)
-    mine = jnp.zeros((8, 128), jnp.int32)
-    for r in range(ROUNDS):
-        mine = jnp.where(index == r, pairings_ref[r, 0], mine)
-        mine = jnp.where(index == ROUNDS + r, subset_ref[r, 0], mine)
-    meta[...] = mine
-
     barrier = pltpu.get_barrier_semaphore()
     everyone = along_x + along_z + [core, low, high]
     for where in everyone:
         pl.semaphore_signal(barrier, inc=1, device_id=where, device_id_type=MESH_ID)
+
+    loads = []
+    moves = ((raw_hbm, raw_ref), (taps_hbm, taps_ref), (slot_hbm, slot_ref), (tables_hbm, tables_ref), (shift_hbm, shift_ref))
+    for n, (src, dst) in enumerate(moves):
+        loads.append(pltpu.make_async_copy(src, dst, load_sem.at[n]))
+        loads[-1].start()
+    index = lax.broadcasted_iota(jnp.int32, (8, 128), 0)
+    mine = jnp.zeros((8, 128), jnp.int32)
+    for r in range(ROUNDS):
+        mine = jnp.where(index == r, pairings_ref[r], mine)
+        mine = jnp.where(index == ROUNDS + r, subset_ref[r], mine)
+    meta[...] = mine
+    whiten_block(
+        raw_ref, taps_ref, slot_ref, tables_ref, shift_ref, panel_ref, filter_ref, dh_ref, dl_ref, re_ref, im_ref, loads
+    )
     pl.semaphore_wait(barrier, len(everyone))
 
     asks = [put(meta, peers.at[0], low), put(meta, peers.at[1], high)]
@@ -214,8 +242,8 @@
     fetch = pltpu.make_async_copy(peers, flat, local)
     fetch.start()
     fetch.wait()
-    my_pair = [pairings_ref[r, 0] for r in range(ROUNDS)]
-    my_sub = [subset_ref[r, 0] for r in range(ROUNDS)]
+    my_pair = [pairings_ref[r] for r in range(ROUNDS)]
+    my_sub = [subset_ref[r] for r in range(ROUNDS)]
     low_sub = [flat[0, ROUNDS + r, 0] for r in range(ROUNDS)]
     high_pair = [flat[1, r, 0] for r in range(ROUNDS)]
 
@@ -280,14 +308,29 @@
 COPIES = 2 + 7 + 3 + 2 + 2 + 14 + 6 + 2 + 2
 
 
-def exchange(panel, pairings, subset):
+def exchange(raw_strain, fir_taps, block_slot, pairings, subset):
     half = (2 * CH, HALF)
+    tables, shift = forward_tables()
     return pl.pallas_call(
         exchange_kernel,
-        out_shape=jax.ShapeDtypeStruct((ROUNDS, 2) + half, BF16),
-        in_specs=[pl.BlockSpec(memory_space=pltpu.SMEM)] * 2 + [pl.BlockSpec(memory_space=pltpu.VMEM)],
-        out_specs=pl.BlockSpec(memory_space=pltpu.VMEM),
+        out_shape=(
+            jax.ShapeDtypeStruct((2,) + half, BF16),
+            jax.ShapeDtypeStruct((ROUNDS, 2) + half, BF16),
+        ),
+        in_specs=[pl.BlockSpec(memory_space=pltpu.SMEM)] * 2 + [pl.BlockSpec(memory_space=pltpu.HBM)] * 5,
+        out_specs=(pl.BlockSpec(memory_space=pltpu.VMEM), pl.BlockSpec(memory_space=pltpu.VMEM)),
         scratch_shapes=[
+            pltpu.VMEM((CH, RAW), F32),
+            pltpu.VMEM((1, TAPS), F32),
+            pltpu.VMEM((1, CH), jnp.int32),
+            pltpu.VMEM((2, PIECE, 2 * NBIN), BF16),
+            pltpu.VMEM((2, PIECES, NBIN), F32),
+            pltpu.VMEM((1, SPAN), F32),
+            pltpu.VMEM((PIECES * CH, PIECE), BF16),
+            pltpu.VMEM((PIECES * CH, PIECE), BF16),
+            pltpu.VMEM((CH, NBIN), F32),
+            pltpu.VMEM((CH, NBIN), F32),
+            pltpu.SemaphoreType.DMA((5,)),
             pltpu.VMEM((8, 128), jnp.int32),
             pltpu.VMEM((2, 8, 128), jnp.int32),
             pltpu.SMEM((2, 8, 128), jnp.int32),
@@ -304,26 +347,13 @@
             pltpu.SemaphoreType.DMA((COPIES,)),
             pltpu.SemaphoreType.DMA,
         ],
-        compiler_params=pltpu.CompilerParams(collective_id=1, has_side_effects=True, vmem_limit_bytes=16 * MIB),
+        compiler_params=pltpu.CompilerParams(collective_id=1, has_side_effects=True, vmem_limit_bytes=GRANT),
         name="exchange",
-    )(pairings, subset, panel)
-
-
-def whiten(raw_strain, fir_taps, block_slot):
-    high, low, tc, ts = forward_tables()
-    taps = jnp.pad(fir_taps, (0, 128 - TAPS)).reshape(1, 128)
-    return pl.pallas_call(
-        whiten_kernel,
-        out_shape=jax.ShapeDtypeStruct((2, 2 * CH, HALF), BF16),
-        in_specs=[pl.BlockSpec(memory_space=pltpu.VMEM)] * 7,
-        out_specs=pl.BlockSpec(memory_space=pltpu.VMEM),
-        scratch_shapes=[pltpu.VMEM((PIECES * CH, PIECE), BF16)] * 2 + [pltpu.VMEM((CH, NBIN), F32)] * 2,
-        compiler_params=pltpu.CompilerParams(vmem_limit_bytes=48 * MIB),
-    )(raw_strain, taps, block_slot.reshape(1, CH), high, low, tc, ts)
+    )(pairings, subset, raw_strain, fir_taps.reshape(1, TAPS), block_slot.reshape(1, CH), tables, shift)
 
 
 def correlate(own, theirs):
-    cosine, sine, turn, flip = lag_tables()
+    lags, turn = lag_tables()
     rows = OWN_STEP * CH
     steps = CH // OWN_STEP
     whole = lambda r, i: (0, 0)
@@ -334,20 +364,25 @@
         in_specs=[
             pl.BlockSpec((2, 2 * CH, HALF), lambda r, i: (0, 0, 0)),
             pl.BlockSpec((1, 2, 2 * CH, HALF), lambda r, i: (r, 0, 0, 0)),
-            pl.BlockSpec((NBIN, LAG), whole),
-            pl.BlockSpec((NBIN, LAG), whole),
+            pl.BlockSpec(memory_space=pltpu.HBM),
             pl.BlockSpec((2, NBIN), whole),
-            pl.BlockSpec((256, 256), whole),
         ],
         out_specs=pl.BlockSpec((rows, 2 * LAG), lambda r, i: (r * steps + i, 0)),
-        scratch_shapes=[pltpu.VMEM((2, CH, NBIN), F32)] + [pltpu.VMEM((rows, NBIN), BF16)] * 2,
-        compiler_params=pltpu.CompilerParams(vmem_limit_bytes=48 * MIB),
-    )(own, theirs, cosine, sine, turn, flip)
+        scratch_shapes=[
+            pltpu.VMEM((2, NBIN, LAG), BF16),
+            pltpu.VMEM((2, CH, NBIN), F32),
+            pltpu.VMEM((rows, NBIN), BF16),
+            pltpu.VMEM((rows, NBIN), BF16),
+            pltpu.SemaphoreType.DMA((2,)),
+        ],
+        compiler_params=pltpu.CompilerParams(vmem_limit_bytes=GRANT),
+    )(own, theirs, lags, turn)
 
 
 def per_device(raw_strain, fir_taps, block_slot, pairings, pair_subset):
-    panel = whiten(raw_strain, fir_taps, block_slot)
-    theirs = exchange(panel, pairings, pair_subset.reshape(ROUNDS, 1))
+    panel, theirs = exchange(
+        raw_strain, fir_taps, block_slot, pairings.reshape(ROUNDS), pair_subset.reshape(ROUNDS)
+    )
     result = correlate(panel, theirs)
     return result.reshape(ROUNDS, KSUB, CH, CH, 2 * LAG)
 

time: 69.5 us -> 59.2 us (0.85)
  local copies, waits for them, and re-layouts: 9.6 us -> 0 us
    unnamed x21 -> x0, local copies, waits for them, and re-layouts: 8.05 us -> none
    reshape x2 -> x0, local copies, waits for them, and re-layouts: 1.55 us -> none  [the longest x1 0.81 us: whiten(): taps = jnp.pad(fir_taps, (0, 128 - TAPS)).reshape(1, 128)]
    pallas_call x1, Pallas kernels: 21.9 us -> 20.9 us  [correlate(): pl.pallas_call(correlate_kernel, grid=(ROUNDS, steps), out_shape=jax.Shap...]
    pallas_call x2 -> x1, Pallas kernels: 37.5 us -> 38.1 us  [exchange(): pl.pallas_call(exchange_kernel, out_shape=(jax.ShapeDtypeStruct((2,) + ha...]
where the time goes in v2:
time: 59.2 us; the launch traced here: 59 us
  Pallas kernels  59 us (100%)
    pallas_call x1, Pallas kernels, exchange(): pl.pallas_call(exchange_kernel, out_shape=(jax.ShapeDtypeStruct((2,) + ha...  38.1 us
    pallas_call x1, Pallas kernels, correlate(): pl.pallas_call(correlate_kernel, grid=(ROUNDS, steps), out_shape=jax.Shap...  20.9 us

profile of v2, /device:TPU:0, one launch (start us, length us, event | category | flops | bytes accessed | tf_op | source)
XLA Modules:
  0.0 59.0 jit_solution(11201350678331727923)
XLA Ops:
  0.0 38.1 %exchange.1 = (bf16[2,80,512]{2,1,0:T(8,128)(2,1)}, bf16[2,2,80,512]{3,2,1,0:T(8,128)(2,1)}) custom-call(s32[2]{0:T(128)} %bitcast.7, s32[2]{0:T(128)} %bitcast.8, f32[40,4160]{1,0:T(8,128)} %raw_hbm.1, f32[1,64]{1,0:T(1,128)} %bitcast.9, s32[1,40]{1,0:T(1,128)} %bitcast.10, bf16[2,256,2048]{2,1,0:T(8,128)(2,1)} %constant.8.clone.tables_hbm, ...), custom_call_target="tpu_custom_call" | custom-call | tf_op jit(solution)/shard_map/exchange/pallas_call | solution.py:314
  38.1 20.9 %shard_map.91 = bf16[3200,2048]{1,0:T(8,128)(2,1)} custom-call(bf16[2,80,512]{2,1,0:T(8,128)(2,1)} %get-tuple-element.7.own_ref, bf16[2,2,80,512]{3,2,1,0:T(8,128)(2,1)} %get-tuple-element.8.their_ref, bf16[2,1024,1024]{2,1,0:T(8,128)(2,1)} %constant.10.clone.lag_hbm, f32[2,1024]{1,0:T(2,128)} %constant.11.clone.turn_ref), custom_call_target="tpu_custom_call" | custom-call | tf_op jit(solution)/shard_map/pallas_call | solution.py:360

commit v3 on v2

--- a/solution.py
+++ b/solution.py
@@ -28,7 +28,11 @@
 SPAN = 640
 OWN_STEP = 8
 MIB = 1 << 20
+CLASSES = (0, 2, 1, 3)
+QUARTER = NBIN // 4
 GRANT = 63 * MIB
+CHUNKS = 4
+BINS = NBIN // CHUNKS
 BF16 = jnp.bfloat16
 F32 = jnp.float32
 
@@ -39,8 +43,12 @@
     return high, low
 
 
+def bin_order():
+    return np.concatenate([np.arange(r, NBIN, 4) for r in CLASSES])
+
+
 def forward_tables():
-    bins = F0 + np.arange(NBIN)
+    bins = F0 + bin_order()
     phases = np.arange(PIECE)[:, None] * bins[None, :] % NFFT * (2.0 * math.pi / NFFT)
     high, low = split_bf16(np.concatenate([np.cos(phases), -np.sin(phases)], axis=1))
     shift = np.arange(PIECES)[:, None] * PIECE * bins[None, :] % NFFT * (2.0 * math.pi / NFFT)
@@ -48,7 +56,7 @@
 
 
 def lag_tables():
-    bins = F0 + np.arange(NBIN)
+    bins = F0 + bin_order()
     phases = bins[:, None] * (2 * np.arange(LAG) + 1)[None, :] % (2 * NFFT) * (math.pi / NFFT)
     scale = 1.0 / math.sqrt(NBIN)
     cosine = (np.cos(phases) * scale).astype(ml_dtypes.bfloat16)
@@ -108,28 +116,38 @@
         re_ref[:, cols] = re
         im_ref[:, cols] = im
     re, im = re_ref[...], im_ref[...]
-    total = re * re + im * im
-    for step in (1, 2, 4, 8, 16, 32):
-        total = total + pltpu.roll(total, NBIN - step, 1)
-    total = pltpu.roll(total, WIN // 2, 1)
-    col = lax.broadcasted_iota(jnp.int32, (CH, NBIN), 1)
-    first, final = WIN // 2, NBIN - WIN // 2
-    total = jnp.where(col < first, total[:, first : first + 1], total)
-    total = jnp.where(col > final, total[:, final : final + 1], total)
-    inverse = lax.rsqrt(total * (1.0 / WIN) + EPS)
+    power = re * re + im * im
+    sums = {}
+    for place_of, r in enumerate(CLASSES):
+        total = power[:, QUARTER * place_of : QUARTER * (place_of + 1)]
+        for step in (1, 2, 4, 8):
+            total = total + pltpu.roll(total, QUARTER - step, 1)
+        sums[r] = total
+    later = {r: pltpu.roll(sums[r], QUARTER - 1, 1) for r in range(3)}
+    col = lax.broadcasted_iota(jnp.int32, (CH, QUARTER), 1)
+    edge = WIN // 8
+    whole = sums[0] + sums[1] + sums[2] + sums[3]
+    first, final = whole[:, :1], whole[:, QUARTER - 2 * edge : QUARTER - 2 * edge + 1]
+    bands = []
+    for r in CLASSES:
+        total = sum(later[n] if n < r else sums[n] for n in range(4))
+        total = pltpu.roll(total, edge, 1)
+        total = jnp.where(col < edge, first, total)
+        bands.append(jnp.where(col >= QUARTER - edge, final, total))
+    inverse = lax.rsqrt(jnp.concatenate(bands, axis=1) * (1.0 / WIN) + EPS)
     place = (lax.broadcasted_iota(jnp.int32, (CH, CH), 0) == slot_ref[...]).astype(F32).astype(BF16)
     re = dot(place, (re * inverse).astype(BF16))
     im = dot(place, (im * inverse).astype(BF16))
-    for n in range(2):
-        cols = slice(HALF * n, HALF * (n + 1))
+    for n in range(CHUNKS):
+        cols = slice(BINS * n, BINS * (n + 1))
         panel_ref[n] = jnp.concatenate([re[:, cols], im[:, cols]], axis=0).astype(BF16)
 
 
 def whole_bins(panel):
     wide = panel.astype(F32)
     return (
-        jnp.concatenate([wide[0, :CH], wide[1, :CH]], axis=1),
-        jnp.concatenate([wide[0, CH:], wide[1, CH:]], axis=1),
+        jnp.concatenate([wide[n, :CH] for n in range(CHUNKS)], axis=1),
+        jnp.concatenate([wide[n, CH:] for n in range(CHUNKS)], axis=1),
     )
 
 
@@ -160,21 +178,41 @@
         rows = slice(CH * i, CH * (i + 2))
         cre_ref[rows, :] = jnp.concatenate(res, axis=0).astype(BF16)
         cim_ref[rows, :] = jnp.concatenate(ims, axis=0).astype(BF16)
+    lag_rows(cre_ref, cim_ref, lag_ref, out_ref)
+
+
+def lag_rows(cre_ref, cim_ref, lag_ref, out_ref):
+    quarters = slice(0, QUARTER), slice(QUARTER, 2 * QUARTER), slice(2 * QUARTER, NBIN)
     backwards = 127 - lax.broadcasted_iota(jnp.int32, (OWN_STEP * CH, 128), 1)
-    width = 512
-    for n in range(LAG // width):
-        cols = slice(width * n, width * (n + 1))
-        even = dot(cre_ref[...], lag_ref[0, :, cols])
-        odd = dot(cim_ref[...], lag_ref[1, :, cols])
-        out_ref[:, LAG + width * n : LAG + width * (n + 1)] = (even + odd).astype(BF16)
-        for q in range(width // 128):
-            piece = even[:, 128 * q : 128 * (q + 1)] - odd[:, 128 * q : 128 * (q + 1)]
-            piece = jnp.take_along_axis(piece, backwards, axis=1, mode="promise_in_bounds")
-            low = LAG - width * n - 128 * (q + 1)
-            out_ref[:, low : low + 128] = piece.astype(BF16)
-
-
-HALF = NBIN // 2
+
+    def mirror(value, low):
+        for n in range(width // 128):
+            piece = jnp.take_along_axis(value[:, 128 * n : 128 * (n + 1)], backwards, axis=1, mode="promise_in_bounds")
+            yield slice(low + width - 128 * (n + 1), low + width - 128 * n), piece
+
+    width = 256
+    half = LAG // 2
+    for n in range(half // width):
+        near = slice(width * n, width * (n + 1))
+        far = slice(LAG - width * (n + 1), LAG - width * n)
+        even = [dot(cre_ref[:, rows], lag_ref[0, rows, near]) for rows in quarters[:2]]
+        odd = [dot(cim_ref[:, rows], lag_ref[1, rows, near]) for rows in quarters[:2]]
+        even_near = even[0] + even[1] + dot(cre_ref[:, quarters[2]], lag_ref[0, quarters[2], near])
+        odd_near = odd[0] + odd[1] + dot(cim_ref[:, quarters[2]], lag_ref[1, quarters[2], near])
+        out_ref[:, LAG + width * n : LAG + width * (n + 1)] = (even_near + odd_near).astype(BF16)
+        for cols, piece in mirror(even_near - odd_near, LAG - width * (n + 1)):
+            out_ref[:, cols] = piece.astype(BF16)
+        even_far, odd_far = even[0] - even[1], odd[1] - odd[0]
+        even_rest = dot(cre_ref[:, quarters[2]], lag_ref[0, quarters[2], far])
+        odd_rest = dot(cim_ref[:, quarters[2]], lag_ref[1, quarters[2], far])
+        rest = even_rest + odd_rest
+        for cols, piece in mirror(even_far + odd_far, 0):
+            out_ref[:, 2 * LAG - width * (n + 1) + cols.start : 2 * LAG - width * (n + 1) + cols.stop] = (piece + rest[:, cols]).astype(BF16)
+        straight = even_far - odd_far
+        for cols, piece in mirror(even_rest - odd_rest, 0):
+            out_ref[:, width * n + cols.start : width * n + cols.stop] = (piece + straight[:, cols]).astype(BF16)
+
+
 MESH_ID = pl.DeviceIdType.MESH
 
 
@@ -184,8 +222,9 @@
 
 def exchange_kernel(pairings_ref, subset_ref, raw_hbm, taps_hbm, slot_hbm, tables_hbm, shift_hbm, panel_ref, theirs_ref,
                     raw_ref, taps_ref, slot_ref, tables_ref, shift_ref, filter_ref, dh_ref, dl_ref, re_ref, im_ref, load_sem,
-                    meta, peers, flat, row, rows0, rows1, line, lines0, lines1,
-                    row_in, rows_in, line_in, lines_in, row_out, rows_out, line_out, lines_out, send, recv, local):
+                    meta, peers, flat, pair, *rest):
+    shared, single = rest[:CHUNKS], rest[CHUNKS : CHUNKS * (1 + ROUNDS)]
+    send, recv, local = rest[CHUNKS * (1 + ROUNDS) :]
     g, m = lax.axis_index("group"), lax.axis_index("member")
     z, h = g // 2, g % 2
     l, x, c = m // 8, (m // 2) % 4, m % 2
@@ -232,90 +271,113 @@
     pl.semaphore_wait(barrier, len(everyone))
 
     asks = [put(meta, peers.at[0], low), put(meta, peers.at[1], high)]
-    row[k] = panel_ref[0]
-    line[z] = panel_ref[1]
-    row_x = [put(panel_ref.at[0], row.at[k], where) for where in along_x]
-    line_z = [put(panel_ref.at[1], line.at[z], where) for where in along_z]
-    row_c = [put(panel_ref.at[0], row.at[k], core)]
-    for ask in asks:
-        ask.wait_recv()
-    fetch = pltpu.make_async_copy(peers, flat, local)
-    fetch.start()
-    fetch.wait()
     my_pair = [pairings_ref[r] for r in range(ROUNDS)]
     my_sub = [subset_ref[r] for r in range(ROUNDS)]
-    low_sub = [flat[0, ROUNDS + r, 0] for r in range(ROUNDS)]
-    high_pair = [flat[1, r, 0] for r in range(ROUNDS)]
-
-    def slot(dx):
-        return lax.rem(x + dx, 4) * 2 + c
-
-    for copy, dx in zip(row_x, (3, 1, 2)):
-        copy.wait_recv()
-        row_c.append(put(row.at[slot(dx)], row.at[slot(dx)], core))
-    for copy in line_z:
-        copy.wait_recv()
-    rows, lines = (rows0, rows1), (lines0, lines1)
     in_group = [lax.rem(my_pair[r], 2) == h for r in range(ROUNDS)]
     in_member = [my_sub[r] // 8 == l for r in range(ROUNDS)]
     my_z = [my_pair[r] // 2 for r in range(ROUNDS)]
     my_k = [lax.rem(my_sub[r], 8) for r in range(ROUNDS)]
-    line_y = []
+    even, odd = tuple(range(0, CHUNKS, 2)), tuple(range(1, CHUNKS, 2))
+    hers = {}
+    moving = {}
+
+    def read_asks():
+        for ask in asks:
+            ask.wait_recv()
+        fetch = pltpu.make_async_copy(peers, flat, local)
+        fetch.start()
+        fetch.wait()
+        for r in range(ROUNDS):
+            hers["k", r] = lax.rem(flat[0, ROUNDS + r, 0], 8)
+            hers["z", r] = flat[1, r, 0] // 2
+
+    def store(q, r):
+        return shared[q] if r < 0 else single[q * ROUNDS + r]
+
+    def by_row(q, r):
+        return (q % 2 == 0) == (r < 0)
+
+    def slot(dx):
+        return lax.rem(x + dx, 4) * 2 + c
+
+    def gather(q, r):
+        room = store(q, r)
+        if by_row(q, r):
+            own, targets = room.at[k], along_x + [core]
+        else:
+            own, targets = room.at[z], along_z
+        src = own
+        if r < 0:
+            room[k if by_row(q, r) else z] = panel_ref[q]
+            src = panel_ref.at[q]
+        moving[q, r] = [put(src, own, where) for where in targets]
+
+    def forward(q, r):
+        if by_row(q, r):
+            room, copies = store(q, r), moving[q, r]
+            for copy, dx in zip(copies[:3], (3, 1, 2)):
+                copy.wait_recv()
+                got = room.at[slot(dx)]
+                copies.append(put(got, got, core))
+            del copies[:3]
+
+    def ask_pair(q, stage, r):
+        if (q, stage) in moving:
+            for copy in moving.pop((q, stage)):
+                copy.wait_recv()
+        out, into = (0, 1) if stage < 0 else (2, 3)
+        row = by_row(q, stage)
+        pair[q, r, out] = store(q, stage)[hers["k" if row else "z", r]]
+        moving[q, stage, r] = put(pair.at[q, r, out], pair.at[q, r, into], low if row else high)
+
+    def chosen(q, stage, r):
+        moving.pop((q, stage, r)).wait_recv()
+        into = pair[q, r, 1 if stage < 0 else 3]
+        if by_row(q, stage):
+            return choose(in_member[r], store(q, stage)[my_k[r]], into)
+        return choose(in_group[r], store(q, stage)[my_z[r]], into)
+
+    def regroup(q, r):
+        single[q * ROUNDS + r][k if by_row(q, r) else z] = chosen(q, -1, r)
+        gather(q, r)
+
+    def finish(q, r):
+        theirs_ref[r, q] = chosen(q, r, r)
+
+    for q in range(CHUNKS):
+        gather(q, -1)
+    read_asks()
+    for q in even:
+        forward(q, -1)
     for r in range(ROUNDS):
-        line_out[r] = line[high_pair[r] // 2]
-        line_y.append(put(line_out.at[r], line_in.at[r], high))
-    for copy in row_c:
-        copy.wait_recv()
-    row_y = []
+        for q in odd + even:
+            ask_pair(q, -1, r)
     for r in range(ROUNDS):
-        row_out[r] = row[lax.rem(low_sub[r], 8)]
-        row_y.append(put(row_out.at[r], row_in.at[r], low))
-
-    rows_x, rows_c, lines_z = [], [], []
+        for q in odd + even:
+            regroup(q, r)
     for r in range(ROUNDS):
-        line_y[r].wait_recv()
-        rows[r][k] = choose(in_group[r], line[my_z[r]], line_in[r])
-        own = rows[r].at[k]
-        rows_x.append([put(own, own, where) for where in along_x])
-        rows_c.append([put(own, own, core)])
-        row_y[r].wait_recv()
-        lines[r][z] = choose(in_member[r], row[my_k[r]], row_in[r])
-        own = lines[r].at[z]
-        lines_z.append([put(own, own, where) for where in along_z])
-    last_line, last_row = [], []
+        for q in odd:
+            forward(q, r)
+        for q in even + odd:
+            ask_pair(q, r, r)
     for r in range(ROUNDS):
-        for copy, dx in zip(rows_x[r], (3, 1, 2)):
-            copy.wait_recv()
-            got = rows[r].at[slot(dx)]
-            rows_c[r].append(put(got, got, core))
-        for copy in lines_z[r]:
-            copy.wait_recv()
-        lines_out[r] = lines[r][high_pair[r] // 2]
-        last_line.append(put(lines_out.at[r], lines_in.at[r], high))
-        for copy in rows_c[r]:
-            copy.wait_recv()
-        rows_out[r] = rows[r][lax.rem(low_sub[r], 8)]
-        last_row.append(put(rows_out.at[r], rows_in.at[r], low))
-    for r in range(ROUNDS):
-        last_line[r].wait_recv()
-        theirs_ref[r, 0] = choose(in_group[r], lines[r][my_z[r]], lines_in[r])
-        last_row[r].wait_recv()
-        theirs_ref[r, 1] = choose(in_member[r], rows[r][my_k[r]], rows_in[r])
+        for q in even + odd:
+            finish(q, r)
     for copy in started:
         copy.wait_send()
 
 
-COPIES = 2 + 7 + 3 + 2 + 2 + 14 + 6 + 2 + 2
+COPIES = 2 + CHUNKS // 2 * 38
 
 
 def exchange(raw_strain, fir_taps, block_slot, pairings, subset):
-    half = (2 * CH, HALF)
+    part = (2 * CH, BINS)
     tables, shift = forward_tables()
     return pl.pallas_call(
         exchange_kernel,
         out_shape=(
-            jax.ShapeDtypeStruct((2,) + half, BF16),
-            jax.ShapeDtypeStruct((ROUNDS, 2) + half, BF16),
+            jax.ShapeDtypeStruct((CHUNKS,) + part, BF16),
+            jax.ShapeDtypeStruct((ROUNDS, CHUNKS) + part, BF16),
         ),
         in_specs=[pl.BlockSpec(memory_space=pltpu.SMEM)] * 2 + [pl.BlockSpec(memory_space=pltpu.HBM)] * 5,
         out_specs=(pl.BlockSpec(memory_space=pltpu.VMEM), pl.BlockSpec(memory_space=pltpu.VMEM)),
@@ -334,14 +396,10 @@
             pltpu.VMEM((8, 128), jnp.int32),
             pltpu.VMEM((2, 8, 128), jnp.int32),
             pltpu.SMEM((2, 8, 128), jnp.int32),
-            pltpu.VMEM((8,) + half, BF16),
-            pltpu.VMEM((8,) + half, BF16),
-            pltpu.VMEM((8,) + half, BF16),
-            pltpu.VMEM((4,) + half, BF16),
-            pltpu.VMEM((4,) + half, BF16),
-            pltpu.VMEM((4,) + half, BF16),
+            pltpu.VMEM((CHUNKS, ROUNDS, 4) + part, BF16),
         ]
-        + [pltpu.VMEM((ROUNDS,) + half, BF16)] * 8
+        + [pltpu.VMEM((8 if q % 2 == 0 else 4,) + part, BF16) for q in range(CHUNKS)]
+        + [pltpu.VMEM((4 if q % 2 == 0 else 8,) + part, BF16) for q in range(CHUNKS) for r in range(ROUNDS)]
         + [
             pltpu.SemaphoreType.DMA((COPIES,)),
             pltpu.SemaphoreType.DMA((COPIES,)),
@@ -362,8 +420,8 @@
         grid=(ROUNDS, steps),
         out_shape=jax.ShapeDtypeStruct((ROUNDS * CH * CH, 2 * LAG), BF16),
         in_specs=[
-            pl.BlockSpec((2, 2 * CH, HALF), lambda r, i: (0, 0, 0)),
-            pl.BlockSpec((1, 2, 2 * CH, HALF), lambda r, i: (r, 0, 0, 0)),
+            pl.BlockSpec((CHUNKS, 2 * CH, BINS), lambda r, i: (0, 0, 0)),
+            pl.BlockSpec((1, CHUNKS, 2 * CH, BINS), lambda r, i: (r, 0, 0, 0)),
             pl.BlockSpec(memory_space=pltpu.HBM),
             pl.BlockSpec((2, NBIN), whole),
         ],

time: 59.2 us -> 55.4 us (0.936)
  Pallas kernels: 59 us -> 55.3 us
    pallas_call x1, Pallas kernels: 20.9 us -> 18.9 us  [correlate(): pl.pallas_call(correlate_kernel, grid=(ROUNDS, steps), out_shape=jax.Shap...]
    pallas_call x1, Pallas kernels: 38.1 us -> 36.3 us  [exchange(): pl.pallas_call(exchange_kernel, out_shape=(jax.ShapeDtypeStruct((CHUNKS,)...]
where the time goes in v3:
time: 55.4 us; the launch traced here: 55.3 us
  Pallas kernels  55.3 us (100%)
    pallas_call x1, Pallas kernels, exchange(): pl.pallas_call(exchange_kernel, out_shape=(jax.ShapeDtypeStruct((CHUNKS,)...  36.3 us
    pallas_call x1, Pallas kernels, correlate(): pl.pallas_call(correlate_kernel, grid=(ROUNDS, steps), out_shape=jax.Shap...  18.9 us

profile of v3, /device:TPU:0, one launch (start us, length us, event | category | flops | bytes accessed | tf_op | source)
XLA Modules:
  0.0 55.3 jit_solution(1023233415906328825)
XLA Ops:
  0.0 36.3 %exchange.1 = (bf16[4,80,256]{2,1,0:T(8,128)(2,1)}, bf16[2,4,80,256]{3,2,1,0:T(8,128)(2,1)}) custom-call(s32[2]{0:T(128)} %bitcast.7, s32[2]{0:T(128)} %bitcast.8, f32[40,4160]{1,0:T(8,128)} %raw_hbm.1, f32[1,64]{1,0:T(1,128)} %bitcast.9, s32[1,40]{1,0:T(1,128)} %bitcast.10, bf16[2,256,2048]{2,1,0:T(8,128)(2,1)} %constant.8.clone.tables_hbm, ...), custom_call_target="tpu_custom_call" | custom-call | tf_op jit(solution)/shard_map/exchange/pallas_call | solution.py:376
  36.3 18.9 %shard_map.91 = bf16[3200,2048]{1,0:T(8,128)(2,1)} custom-call(bf16[4,80,256]{2,1,0:T(8,128)(2,1)} %get-tuple-element.7.own_ref, bf16[2,4,80,256]{3,2,1,0:T(8,128)(2,1)} %get-tuple-element.8.their_ref, bf16[2,1024,1024]{2,1,0:T(8,128)(2,1)} %constant.10.clone.lag_hbm, f32[2,1024]{1,0:T(2,128)} %constant.11.clone.turn_ref), custom_call_target="tpu_custom_call" | custom-call | tf_op jit(solution)/shard_map/pallas_call | solution.py:418

commit v4 on v3

--- a/solution.py
+++ b/solution.py
@@ -153,7 +153,11 @@
 
 def correlate_kernel(own_ref, their_ref, lag_hbm, turn_ref, out_ref, lag_ref, turned_ref, cre_ref, cim_ref, load_sem):
     first = (pl.program_id(0) == 0) & (pl.program_id(1) == 0)
-    loads = [pltpu.make_async_copy(lag_hbm.at[n], lag_ref.at[n], load_sem.at[n]) for n in range(2)]
+    loads = []
+    for n in range(2):
+        for q in range(4):
+            at = (n, pl.ds(QUARTER * q, QUARTER), pl.ds(0, LAG // 2 if q < 2 else LAG))
+            loads.append(pltpu.make_async_copy(lag_hbm.at[at], lag_ref.at[at], load_sem.at[4 * n + q]))
 
     @pl.when(first)
     def _():
@@ -235,8 +239,8 @@
         member = lax.rem(l + dl, 2) * 8 + lax.rem(x + dx, 4) * 2 + lax.rem(c + dc, 2)
         return group, member
 
-    along_x = [at(dx=d) for d in (1, 3, 2)]
-    along_z = [at(dz=d) for d in (1, 3, 2)]
+    along_x = [at(dx=d) for d in (2, 1, 3)]
+    along_z = [at(dz=d) for d in (2, 1, 3)]
     core, low, high = at(dc=1), at(dl=1), at(dh=1)
     started = []
 
@@ -315,7 +319,7 @@
     def forward(q, r):
         if by_row(q, r):
             room, copies = store(q, r), moving[q, r]
-            for copy, dx in zip(copies[:3], (3, 1, 2)):
+            for copy, dx in zip(copies[:3], (2, 3, 1)):
                 copy.wait_recv()
                 got = room.at[slot(dx)]
                 copies.append(put(got, got, core))
@@ -431,7 +435,7 @@
             pltpu.VMEM((2, CH, NBIN), F32),
             pltpu.VMEM((rows, NBIN), BF16),
             pltpu.VMEM((rows, NBIN), BF16),
-            pltpu.SemaphoreType.DMA((2,)),
+            pltpu.SemaphoreType.DMA((8,)),
         ],
         compiler_params=pltpu.CompilerParams(vmem_limit_bytes=GRANT),
     )(own, theirs, lags, turn)

time: 55.4 us -> 54.9 us (level)
  Pallas kernels: 55.3 us -> 54.7 us
where the time goes in v4:
time: 54.9 us; the launch traced here: 54.7 us
  Pallas kernels  54.7 us (100%)
    pallas_call x1, Pallas kernels, exchange(): pl.pallas_call(exchange_kernel, out_shape=(jax.ShapeDtypeStruct((CHUNKS,)...  36.1 us
    pallas_call x1, Pallas kernels, correlate(): pl.pallas_call(correlate_kernel, grid=(ROUNDS, steps), out_shape=jax.Shap...  18.6 us

profile of v4, /device:TPU:0, one launch (start us, length us, event | category | flops | bytes accessed | tf_op | source)
XLA Modules:
  0.0 54.7 jit_solution(7049560143604024374)
XLA Ops:
  0.0 36.1 %exchange.1 = (bf16[4,80,256]{2,1,0:T(8,128)(2,1)}, bf16[2,4,80,256]{3,2,1,0:T(8,128)(2,1)}) custom-call(s32[2]{0:T(128)} %bitcast.7, s32[2]{0:T(128)} %bitcast.8, f32[40,4160]{1,0:T(8,128)} %raw_hbm.1, f32[1,64]{1,0:T(1,128)} %bitcast.9, s32[1,40]{1,0:T(1,128)} %bitcast.10, bf16[2,256,2048]{2,1,0:T(8,128)(2,1)} %constant.8.clone.tables_hbm, ...), custom_call_target="tpu_custom_call" | custom-call | tf_op jit(solution)/shard_map/exchange/pallas_call | solution.py:380
  36.1 18.6 %shard_map.91 = bf16[3200,2048]{1,0:T(8,128)(2,1)} custom-call(bf16[4,80,256]{2,1,0:T(8,128)(2,1)} %get-tuple-element.7.own_ref, bf16[2,4,80,256]{3,2,1,0:T(8,128)(2,1)} %get-tuple-element.8.their_ref, bf16[2,1024,1024]{2,1,0:T(8,128)(2,1)} %constant.10.clone.lag_hbm, f32[2,1024]{1,0:T(2,128)} %constant.11.clone.turn_ref), custom_call_target="tpu_custom_call" | custom-call | tf_op jit(solution)/shard_map/pallas_call | solution.py:422

commit v5 on v4

--- a/solution.py
+++ b/solution.py
@@ -350,9 +350,9 @@
 
     for q in range(CHUNKS):
         gather(q, -1)
-    read_asks()
     for q in even:
         forward(q, -1)
+    read_asks()
     for r in range(ROUNDS):
         for q in odd + even:
             ask_pair(q, -1, r)

time: 54.9 us -> 56.4 us (1.027)
  Pallas kernels: 54.7 us -> 56.2 us
    pallas_call x1, Pallas kernels: 36.1 us -> 37.6 us  [exchange(): pl.pallas_call(exchange_kernel, out_shape=(jax.ShapeDtypeStruct((CHUNKS,)...]
where the time goes in v5:
time: 56.4 us; the launch traced here: 56.2 us
  Pallas kernels  56.2 us (100%)
    pallas_call x1, Pallas kernels, exchange(): pl.pallas_call(exchange_kernel, out_shape=(jax.ShapeDtypeStruct((CHUNKS,)...  37.6 us
    pallas_call x1, Pallas kernels, correlate(): pl.pallas_call(correlate_kernel, grid=(ROUNDS, steps), out_shape=jax.Shap...  18.6 us

profile of v5, /device:TPU:0, one launch (start us, length us, event | category | flops | bytes accessed | tf_op | source)
XLA Modules:
  0.0 56.2 jit_solution(18198737369159118190)
XLA Ops:
  0.0 37.6 %exchange.1 = (bf16[4,80,256]{2,1,0:T(8,128)(2,1)}, bf16[2,4,80,256]{3,2,1,0:T(8,128)(2,1)}) custom-call(s32[2]{0:T(128)} %bitcast.7, s32[2]{0:T(128)} %bitcast.8, f32[40,4160]{1,0:T(8,128)} %raw_hbm.1, f32[1,64]{1,0:T(1,128)} %bitcast.9, s32[1,40]{1,0:T(1,128)} %bitcast.10, bf16[2,256,2048]{2,1,0:T(8,128)(2,1)} %constant.8.clone.tables_hbm, ...), custom_call_target="tpu_custom_call" | custom-call | tf_op jit(solution)/shard_map/exchange/pallas_call | solution.py:380
  37.6 18.6 %shard_map.91 = bf16[3200,2048]{1,0:T(8,128)(2,1)} custom-call(bf16[4,80,256]{2,1,0:T(8,128)(2,1)} %get-tuple-element.7.own_ref, bf16[2,4,80,256]{3,2,1,0:T(8,128)(2,1)} %get-tuple-element.8.their_ref, bf16[2,1024,1024]{2,1,0:T(8,128)(2,1)} %constant.10.clone.lag_hbm, f32[2,1024]{1,0:T(2,128)} %constant.11.clone.turn_ref), custom_call_target="tpu_custom_call" | custom-call | tf_op jit(solution)/shard_map/pallas_call | solution.py:422
